TPU v7x, 256 devices: a whole 4x4x8 slice. The times are simulated.
256 devices in a mesh: expert: 64 (over x, z, core), fsdp: 4 (over y).
Axes of the slice: x: 4, y: 4, z: 8, core: 2. Of those that a mesh axis runs over, the one named last changes fastest.
Arguments:
- teacher_in: bfloat16 [8192, 4096], P('expert'), may hold values from -6 to 6
- routes: int32 [8192, 8], P('expert'), may hold values from 0 to 63, all different within a row; in each aligned block of 128 rows (0 to 127, 128 to 255, ...) at most 18 rows name the same one
- route_weights: float32 [8192, 8], P('expert'), may hold values from 0.1 to 0.5
- expert_gate_up: bfloat16 [64, 4096, 2, 1024], P('expert', None, None, 'fsdp'), may hold values from -0.09375 to 0.09375
- expert_down: bfloat16 [64, 1024, 4096], P('expert', 'fsdp'), may hold values from -0.1875 to 0.1875
- student_in: bfloat16 [8192, 2048], P('expert'), may hold values from -16 to 16
- norm_gain: float32 [2048], replicated, may hold values from 0.5 to 2
- projector: bfloat16 [2048, 4096], P(None, 'fsdp'), may hold values from -0.125 to 0.125
- second_moment: float32 [2048, 4096], P('expert', 'fsdp'), may hold values from 2048 to 32768
Outputs:
- d_student: bfloat16 [8192, 2048], P('expert')
- proj_step: float32 [2048, 4096], P('expert', 'fsdp')
Inputs may be any that keep to these rules, and one draw needn't show every extreme that they name: `routes`: each row names 8 different experts; in each block of 128 consecutive rows (the rows of one index of expert) no expert is named by more than 18 rows.
All inputs are finite; a program needn't handle non-finite values.
Results may differ from a plain program's by a relative error of at most 0.02.
Values may be sent and summed in bfloat16 or wider, within the bound.
A program may use at most 128 MiB of HBM per device.

v0:
```python
import jax
import jax.numpy as jnp
from jax import lax
from jax.sharding import PartitionSpec as P

beta_two = 0.95


def slot_maps(routes, route_weights, experts):
    tokens = routes.shape[0]
    named = routes[:, :, None] == jnp.arange(experts, dtype=jnp.int32)[None, None, :]
    member = jnp.any(named, axis=1)
    weight = jnp.sum(jnp.where(named, route_weights[:, :, None], 0.0), axis=1)
    earlier = jnp.tril(jnp.ones((tokens, tokens), jnp.bfloat16), -1)
    before = jnp.dot(earlier, member.astype(jnp.bfloat16), preferred_element_type=jnp.float32)
    position = jnp.where(member, before.astype(jnp.int32), -1)
    return (position.T, weight.T)


def per_device(
    teacher_in,
    routes,
    route_weights,
    expert_gate_up,
    expert_down,
    student_in,
    norm_gain,
    projector,
    second_moment,
):
    tokens_here, model_width = teacher_in.shape
    top_count = routes.shape[1]
    experts = lax.axis_size("expert")
    shares = lax.axis_size("fsdp")
    part = model_width // shares
    capacity = min(tokens_here, tokens_here * top_count * 9 // (8 * experts))
    position, weight = slot_maps(routes, route_weights, experts)
    onehot = position[:, None, :] == jnp.arange(capacity, dtype=jnp.int32)[None, :, None]
    select = onehot.astype(jnp.bfloat16)
    weighted = jnp.where(onehot, weight[:, None, :], 0.0)
    high = weighted.astype(jnp.bfloat16)
    low = (weighted - high.astype(jnp.float32)).astype(jnp.bfloat16)
    mine = lax.axis_index("fsdp") * part
    columns = lax.dynamic_slice_in_dim(teacher_in, mine, part, axis=1)
    buffer = jnp.einsum("est,tc->esc", select, columns, preferred_element_type=jnp.float32)
    buffer = buffer.astype(jnp.bfloat16)
    received = lax.all_to_all(buffer, "expert", split_axis=0, concat_axis=0, tiled=True)
    rows = lax.all_gather(received, "fsdp", axis=0)
    down_rows = lax.all_to_all(expert_down[0], "fsdp", split_axis=1, concat_axis=0, tiled=True)
    gate_up = expert_gate_up.reshape(shares, part, -1)
    gate_up_out = jnp.einsum("yesc,ycn->esn", rows, gate_up, preferred_element_type=jnp.float32)
    half = gate_up_out.shape[2] // 2
    hidden = (jax.nn.silu(gate_up_out[:, :, :half]) * gate_up_out[:, :, half:]).astype(jnp.bfloat16)
    hidden_all = lax.all_gather(hidden, "fsdp", axis=0)
    expert_out = jnp.einsum(
        "yesh,yhc->esc",
        hidden_all,
        down_rows.reshape(shares, half, part),
        preferred_element_type=jnp.float32,
    )
    returned = lax.all_to_all(
        expert_out.astype(jnp.bfloat16), "expert", split_axis=0, concat_axis=0, tiled=True
    )
    teacher = jnp.einsum(
        "est,esc->tc", high, returned, preferred_element_type=jnp.float32
    ) + jnp.einsum("est,esc->tc", low, returned, preferred_element_type=jnp.float32)
    student_wide = student_in.astype(jnp.float32)
    inv_rms = lax.rsqrt(jnp.mean(student_wide * student_wide, axis=1, keepdims=True) + 1e-06)
    normed = student_wide * inv_rms
    student_feat = (normed * norm_gain[None, :]).astype(jnp.bfloat16)
    residue = (
        jnp.dot(student_feat, projector, preferred_element_type=jnp.float32) - teacher
    ).astype(jnp.bfloat16)
    feat_part = jnp.einsum("tc,dc->td", residue, projector, preferred_element_type=jnp.float32)
    feat_grad = lax.psum(feat_part.astype(jnp.bfloat16), "fsdp").astype(jnp.float32)
    scaled = feat_grad * norm_gain[None, :]
    d_student = (
        inv_rms * (scaled - normed * jnp.mean(scaled * normed, axis=1, keepdims=True))
    ).astype(jnp.bfloat16)
    grad_block = lax.psum_scatter(
        jnp.einsum("tr,tc->rc", student_feat, residue, preferred_element_type=jnp.float32),
        "expert",
        scatter_dimension=0,
        tiled=True,
    )
    proj_step = grad_block / jnp.sqrt(
        beta_two * second_moment + (1.0 - beta_two) * grad_block * grad_block
    )
    return (d_student, proj_step)


def solution(mesh):
    placed = (
        P("expert", None),
        P("expert", None),
        P("expert", None),
        P("expert", None, None, "fsdp"),
        P("expert", "fsdp", None),
        P("expert", None),
        P(),
        P(None, "fsdp"),
        P("expert", "fsdp"),
    )
    return jax.shard_map(
        per_device,
        mesh=mesh,
        in_specs=placed,
        out_specs=(P("expert", None), P("expert", "fsdp")),
        check_vma=False,
    )
```

profile of v0, /device:TPU:8, one launch (start us, length us, event | category | flops | bytes accessed | tf_op | source)
XLA Modules:
  0.0 567.9 jit_solution(15985997728687819142)
XLA Ops:
  7.2 0.8 fusion.37
  8.0 0.2 fusion.19
  8.3 0.2 copy-done
  8.4 0.8 convolution_convert_fusion.1
  9.2 1.4 copy.35
  10.6 84.8 %all_to_all.26 = bf16[64,18,1024]{2,1,0:T(8,128)(2,1)S(1)} all-to-all(bf16[64,18,1024]{2,1,0:T(8,128)(2,1)S(1)} %copy.35), channel_id=1, replica_groups=mesh['expert'=64,'fsdp'=4] {'expert'}, dimensions={0} | all-to-all | bytes 4718592 | tf_op jit(solution)/shard_map/all_to_all | solution.py:47
  95.4 2.7 copy.36
  98.1 0.0 all-gather.7.cloned.1.call-start
  98.1 7.6 %reshape.34 = bf16[4,1024,512,1]{2,1,0,3:T(8,128)(2,1)} reshape(bf16[1,4096,2,256]{3,2,1,0:T(2,128)(2,1)} %param.12) | data formatting | bytes 8388608 | tf_op jit(solution)/shard_map/reshape | solution.py:50
  105.7 84.6 %all-gather.5.cloned.1.call-done = bf16[256,18,1024]{2,0,1:T(8,128)(2,1)} async-done(((bf16[64,18,1024]{2,0,1:T(8,128)(2,1)}), bf16[256,18,1024]{2,0,1:T(8,128)(2,1)}) %all-gather.5.cloned.1.call-update) | async-done | bytes 9437200 | tf_op jit(solution)/shard_map/all_gather | solution.py:48
  190.3 8.8 %convolution_bitcast_fusion = f32[64,18,512]{2,0,1:T(8,128)S(1)} fusion(bf16[4,64,18,1024]{3,1,0,2:T(8,128)(2,1)} %bitcast.37, bf16[4,1024,512,1]{2,1,0,3:T(8,128)(2,1)} %reshape.34), kind=kOutput, calls=%fused_computation.4 | convolution fusion | flops 4831838208 | bytes 15990784 | tf_op jit(solution)/shard_map/yesc,ycn->esn/dot_general | solution.py:51
  199.2 1.2 fusion.18
  200.4 0.6 copy-done.4
  201.0 2.4 copy.37
  203.4 3.0 copy.38
  206.4 48.3 %all_to_all.27 = bf16[256,4,1024]{2,0,1:T(8,128)(2,1)} all-to-all(bf16[256,4,1024]{2,0,1:T(8,128)(2,1)S(1)} %copy.38), channel_id=1, replica_groups=mesh['expert'=64,'fsdp'=4] {'fsdp'}, dimensions={1} | all-to-all | bytes 4194304 | tf_op jit(solution)/shard_map/all_to_all | solution.py:49
  254.7 4.9 bitcast_convert_fusion
  259.6 3.1 copy.39
  262.7 10.8 %all-to-all-start.2 = ((bf16[64,18,1024]{2,1,0:T(8,128)(2,1)}), bf16[64,18,1024]{2,1,0:T(8,128)(2,1)}, u32[]{:S(2)}, u32[]{:S(2)}) async-start(bf16[64,18,1024]{2,1,0:T(8,128)(2,1)} %copy.39), calls=%async_computation.2 | async-start | bytes 6291456 | tf_op jit(solution)/shard_map/all_to_all | solution.py:61
  273.6 0.2 fusion.25
  273.8 72.9 %all-to-all-done.2 = bf16[64,18,1024]{2,1,0:T(8,128)(2,1)} async-done(((bf16[64,18,1024]{2,1,0:T(8,128)(2,1)}), bf16[64,18,1024]{2,1,0:T(8,128)(2,1)}, u32[]{:S(2)}, u32[]{:S(2)}) %all-to-all-start.2) | async-done | bytes 2359328 | tf_op jit(solution)/shard_map/all_to_all | solution.py:61
  346.7 4.8 fusion.8
  351.5 4.7 fusion.14
  356.2 0.8 fusion.17
  357.1 2.3 convolution_convert_fusion
  359.4 0.0 reduce-scatter.2.cloned.1.call-start
  359.4 4.6 fusion.38
  364.1 38.8 %all-reduce.2.cloned.1.call-done = bf16[128,2048]{1,0:T(8,128)(2,1)} async-done(((bf16[128,2048]{1,0:T(8,128)(2,1)}), bf16[128,2048]{1,0:T(8,128)(2,1)}) %all-reduce.2.cloned.1.call-update) | async-done | bytes 524304 | tf_op jit(solution)/shard_map/psum | solution.py:75
  402.9 1.4 fusion.21
  404.3 2.2 fusion.24
  406.5 153.3 %reduce-scatter.2.cloned.1.call-done = f32[32,1024]{1,0:T(8,128)} async-done(((f32[2048,1024]{1,0:T(8,128)}), f32[32,1024]{1,0:T(8,128)}) %reduce-scatter.2.cloned.1.call-update) | async-done | bytes 131088 | tf_op jit(solution)/shard_map/reduce_scatter | solution.py:80
  559.8 1.6 fusion.43
  (27 shorter events, 0.2 us)
Async XLA Ops:
  7.2 1.2 copy-start
  7.2 183.2 %all-gather.5.cloned.1.call-start = ((), (), s32[]{:S(2)}) async-start(), calls=%async_computation.6 | async-start | bytes 11796480 | tf_op jit(solution)/shard_map/all_gather | solution.py:48
  98.1 156.6 %all-gather.7.cloned.1.call-start = ((), (), s32[]{:S(2)}) async-start(), calls=%async_computation.7 | async-start | bytes 2949120 | tf_op jit(solution)/shard_map/all_gather | solution.py:54
  199.2 1.8 copy-start.4
  262.7 10.9 %copy-start.7 = (s32[128,8]{0,1:T(8,128)S(1)}, s32[128,8]{0,1:T(8,128)}, u32[]{:S(2)}) copy-start(s32[128,8]{0,1:T(8,128)} %param.10) | copy-start | bytes 12292
  262.7 10.9 %copy-start.8 = (f32[128,8]{0,1:T(8,128)S(1)}, f32[128,8]{0,1:T(8,128)}, u32[]{:S(2)}) copy-start(f32[128,8]{0,1:T(8,128)} %param.11) | copy-start | bytes 12292
  262.7 10.9 %copy-start.3 = (bf16[128,2048]{1,0:T(8,128)(2,1)S(1)}, bf16[128,2048]{1,0:T(8,128)(2,1)}, u32[]{:S(2)}) copy-start(bf16[128,2048]{1,0:T(8,128)(2,1)} %param.14) | copy-start | bytes 1572868
  262.7 84.0 %all-to-all-start.2 = ((bf16[64,18,1024]{2,1,0:T(8,128)(2,1)}), bf16[64,18,1024]{2,1,0:T(8,128)(2,1)}, u32[]{:S(2)}, u32[]{:S(2)}) async-start(bf16[64,18,1024]{2,1,0:T(8,128)(2,1)} %copy.39), calls=%async_computation.2 | async-start | bytes 6291456 | tf_op jit(solution)/shard_map/all_to_all | solution.py:61
  273.5 129.4 %all-reduce.2.cloned.1.call-start = ((), (), s32[]{:S(2)}) async-start(), calls=%async_computation.4 | async-start | bytes 1048576 | tf_op jit(solution)/shard_map/psum | solution.py:75
  346.7 9.5 %copy-start.2 = (bf16[2048,1024]{1,0:T(8,128)(2,1)S(1)}, bf16[2048,1024]{1,0:T(8,128)(2,1)}, u32[]{:S(2)}) copy-start(bf16[2048,1024]{1,0:T(8,128)(2,1)} %param.16) | copy-start | bytes 12582916
  351.5 4.7 copy-start.5
  359.4 200.4 %reduce-scatter.2.cloned.1.call-start = ((), (), s32[]{:S(2)}) async-start(), calls=%async_computation.5 | async-start | bytes 8519680 | tf_op jit(solution)/shard_map/reduce_scatter | solution.py:80
  364.1 195.8 %copy-start.6 = (f32[32,1024]{1,0:T(8,128)S(1)}, f32[32,1024]{1,0:T(8,128)}, u32[]{:S(2)}) copy-start(f32[32,1024]{1,0:T(8,128)} %param.17) | copy-start | bytes 393220
  364.1 197.3 %copy-start.1 = (bf16[128,4096]{1,0:T(8,128)(2,1)S(1)}, bf16[128,4096]{1,0:T(8,128)(2,1)}, u32[]{:S(2)}) copy-start(bf16[128,4096]{1,0:T(8,128)(2,1)} %param.9) | copy-start | bytes 3145732
Sparse Core Ops, SparseCore 0:
  98.2 92.1 all-gather.4
  200.5 53.4 all-gather.6
  359.5 43.3 all-reduce.1
  407.0 152.7 reduce-scatter.1
where the time goes:
time: 569 us; the launch traced here: 568 us
  waiting for transfers between devices  350 us (62%)
  blocking collectives  133 us (23%)
  matrix products  31.9 us (6%)
  local copies, waits for them, and re-layouts  20.9 us (4%)
  between operations  13.9 us (2%)
  starting transfers between devices  11 us (2%)
  other arithmetic  7.36 us (1%)
    reduce_scatter x1, waiting for transfers between devices, per_device(): lax.psum_scatter(jnp.einsum('tr,tc->rc', student_feat, residue, preferred...  153 us
    all_to_all x1, blocking collectives, per_device(): lax.all_to_all(buffer, 'expert', split_axis=0, concat_axis=0, tiled=True)  84.8 us
    all_gather x1, waiting for transfers between devices, per_device(): rows = lax.all_gather(received, 'fsdp', axis=0)  84.6 us
    all_to_all x1, waiting for transfers between devices, per_device(): lax.all_to_all(expert_out.astype(jnp.bfloat16), 'expert', split_axis=0, c...  72.9 us
    all_to_all x1, blocking collectives, per_device(): lax.all_to_all(expert_down[0], 'fsdp', split_axis=1, concat_axis=0, tiled...  48.3 us
    psum x1, waiting for transfers between devices, per_device(): lax.psum(feat_part.astype(jnp.bfloat16), 'fsdp').astype(jnp.float32)  38.8 us
  transfers between devices with their start and end apart: 5, of which 4 were waited for; matrix products, arithmetic and copies ran while one was open for 4% of the time, Pallas kernels for 0%

commit v1 on v0

--- a/solution.py
+++ b/solution.py
@@ -4,6 +4,11 @@
 from jax.sharding import PartitionSpec as P
 
 beta_two = 0.95
+
+
+def gather_and_add(x, name):
+    shards = lax.all_gather(x, name)
+    return jnp.sum(shards, axis=0)
 
 
 def slot_maps(routes, route_weights, experts):
@@ -72,7 +77,7 @@
         jnp.dot(student_feat, projector, preferred_element_type=jnp.float32) - teacher
     ).astype(jnp.bfloat16)
     feat_part = jnp.einsum("tc,dc->td", residue, projector, preferred_element_type=jnp.float32)
-    feat_grad = lax.psum(feat_part.astype(jnp.bfloat16), "fsdp").astype(jnp.float32)
+    feat_grad = gather_and_add(feat_part.astype(jnp.bfloat16), "fsdp").astype(jnp.float32)
     scaled = feat_grad * norm_gain[None, :]
     d_student = (
         inv_rms * (scaled - normed * jnp.mean(scaled * normed, axis=1, keepdims=True))

time: 569 us -> 554 us (0.974)
  waiting for transfers between devices: 350 us -> 335 us
    psum x1 -> x0, waiting for transfers between devices: 38.8 us -> none  [per_device(): lax.psum(feat_part.astype(jnp.bfloat16), 'fsdp').astype(jnp.float32)]
    all_gather x0 -> x1, waiting for transfers between devices: none -> 24.2 us  [gather_and_add(): shards = lax.all_gather(x, name)]
where the time goes in v1:
time: 554 us; the launch traced here: 553 us
  waiting for transfers between devices  335 us (60%)
  blocking collectives  133 us (24%)
  matrix products  31.9 us (6%)
  local copies, waits for them, and re-layouts  20.9 us (4%)
  between operations  13.9 us (3%)
  starting transfers between devices  11 us (2%)
  other arithmetic  7.4 us (1%)
    reduce_scatter x1, waiting for transfers between devices, per_device(): lax.psum_scatter(jnp.einsum('tr,tc->rc', student_feat, residue, preferred...  153 us
    all_to_all x1, blocking collectives, per_device(): lax.all_to_all(buffer, 'expert', split_axis=0, concat_axis=0, tiled=True)  84.8 us
    all_gather x1, waiting for transfers between devices, per_device(): rows = lax.all_gather(received, 'fsdp', axis=0)  84.6 us
    all_to_all x1, waiting for transfers between devices, per_device(): lax.all_to_all(expert_out.astype(jnp.bfloat16), 'expert', split_axis=0, c...  72.9 us
    all_to_all x1, blocking collectives, per_device(): lax.all_to_all(expert_down[0], 'fsdp', split_axis=1, concat_axis=0, tiled...  48.3 us
    all_gather x1, waiting for transfers between devices, gather_and_add(): shards = lax.all_gather(x, name)  24.2 us
  transfers between devices with their start and end apart: 5, of which 4 were waited for; matrix products, arithmetic and copies ran while one was open for 4% of the time, Pallas kernels for 0%

profile of v1, /device:TPU:8, one launch (start us, length us, event | category | flops | bytes accessed | tf_op | source)
XLA Modules:
  0.0 553.0 jit_solution(15871186206869330192)
XLA Ops:
  7.2 0.8 fusion.37
  8.0 0.2 fusion.19
  8.3 0.2 copy-done
  8.4 0.8 convolution_convert_fusion.1
  9.2 1.4 copy.35
  10.6 84.8 %all_to_all.26 = bf16[64,18,1024]{2,1,0:T(8,128)(2,1)S(1)} all-to-all(bf16[64,18,1024]{2,1,0:T(8,128)(2,1)S(1)} %copy.35), channel_id=1, replica_groups=mesh['expert'=64,'fsdp'=4] {'expert'}, dimensions={0} | all-to-all | bytes 4718592 | tf_op jit(solution)/shard_map/all_to_all | solution.py:52
  95.4 2.7 copy.36
  98.1 7.6 %reshape.35 = bf16[4,1024,512,1]{2,1,0,3:T(8,128)(2,1)} reshape(bf16[1,4096,2,256]{3,2,1,0:T(2,128)(2,1)} %param.12) | data formatting | bytes 8388608 | tf_op jit(solution)/shard_map/reshape | solution.py:55
  105.7 84.6 %all-gather.7.cloned.1.call-done = bf16[256,18,1024]{2,0,1:T(8,128)(2,1)} async-done(((bf16[64,18,1024]{2,0,1:T(8,128)(2,1)}), bf16[256,18,1024]{2,0,1:T(8,128)(2,1)}) %all-gather.7.cloned.1.call-update) | async-done | bytes 9437200 | tf_op jit(solution)/shard_map/all_gather | solution.py:53
  190.3 8.8 %convolution_bitcast_fusion = f32[64,18,512]{2,0,1:T(8,128)S(1)} fusion(bf16[4,64,18,1024]{3,1,0,2:T(8,128)(2,1)} %bitcast.39, bf16[4,1024,512,1]{2,1,0,3:T(8,128)(2,1)} %reshape.35), kind=kOutput, calls=%fused_computation.4 | convolution fusion | flops 4831838208 | bytes 15990784 | tf_op jit(solution)/shard_map/yesc,ycn->esn/dot_general | solution.py:56
  199.2 1.2 fusion.18
  200.4 0.6 copy-done.4
  201.0 2.4 copy.37
  203.4 3.0 copy.38
  206.4 48.3 %all_to_all.27 = bf16[256,4,1024]{2,0,1:T(8,128)(2,1)} all-to-all(bf16[256,4,1024]{2,0,1:T(8,128)(2,1)S(1)} %copy.38), channel_id=1, replica_groups=mesh['expert'=64,'fsdp'=4] {'fsdp'}, dimensions={1} | all-to-all | bytes 4194304 | tf_op jit(solution)/shard_map/all_to_all | solution.py:54
  254.7 4.9 bitcast_convert_fusion
  259.6 3.1 copy.39
  262.7 10.8 %all-to-all-start.2 = ((bf16[64,18,1024]{2,1,0:T(8,128)(2,1)}), bf16[64,18,1024]{2,1,0:T(8,128)(2,1)}, u32[]{:S(2)}, u32[]{:S(2)}) async-start(bf16[64,18,1024]{2,1,0:T(8,128)(2,1)} %copy.39), calls=%async_computation.2 | async-start | bytes 6291456 | tf_op jit(solution)/shard_map/all_to_all | solution.py:66
  273.5 0.0 all-gather.11.cloned.1.call-start
  273.6 0.2 fusion.25
  273.8 72.9 %all-to-all-done.2 = bf16[64,18,1024]{2,1,0:T(8,128)(2,1)} async-done(((bf16[64,18,1024]{2,1,0:T(8,128)(2,1)}), bf16[64,18,1024]{2,1,0:T(8,128)(2,1)}, u32[]{:S(2)}, u32[]{:S(2)}) %all-to-all-start.2) | async-done | bytes 2359328 | tf_op jit(solution)/shard_map/all_to_all | solution.py:66
  346.7 4.8 fusion.8
  351.5 4.7 fusion.14
  356.2 0.8 fusion.17
  357.1 2.3 convolution_convert_fusion
  359.4 4.6 fusion.38
  364.1 24.2 %all-gather.11.cloned.1.call-done = bf16[512,2048]{1,0:T(8,128)(2,1)} async-done(((bf16[128,2048]{1,0:T(8,128)(2,1)}), bf16[512,2048]{1,0:T(8,128)(2,1)}) %all-gather.11.cloned.1.call-update) | async-done | bytes 2097168 | tf_op jit(solution)/shard_map/all_gather | solution.py:10
  388.2 2.1 reduce_sum.41
  390.3 0.3 fusion.21
  390.7 1.2 fusion.24
  391.8 153.1 %reduce-scatter.2.cloned.1.call-done = f32[32,1024]{1,0:T(8,128)} async-done(((f32[2048,1024]{1,0:T(8,128)}), f32[32,1024]{1,0:T(8,128)}) %reduce-scatter.2.cloned.1.call-update) | async-done | bytes 131088 | tf_op jit(solution)/shard_map/reduce_scatter | solution.py:85
  544.9 1.6 fusion.43
  (28 shorter events, 0.3 us)
Async XLA Ops:
  7.2 1.2 copy-start
  7.2 183.2 %all-gather.7.cloned.1.call-start = ((), (), s32[]{:S(2)}) async-start(), calls=%async_computation.5 | async-start | bytes 11796480 | tf_op jit(solution)/shard_map/all_gather | solution.py:53
  98.1 156.6 %all-gather.9.cloned.1.call-start = ((), (), s32[]{:S(2)}) async-start(), calls=%async_computation.6 | async-start | bytes 2949120 | tf_op jit(solution)/shard_map/all_gather | solution.py:59
  199.2 1.8 copy-start.4
  262.7 10.9 %copy-start.7 = (s32[128,8]{0,1:T(8,128)S(1)}, s32[128,8]{0,1:T(8,128)}, u32[]{:S(2)}) copy-start(s32[128,8]{0,1:T(8,128)} %param.10) | copy-start | bytes 12292
  262.7 10.9 %copy-start.8 = (f32[128,8]{0,1:T(8,128)S(1)}, f32[128,8]{0,1:T(8,128)}, u32[]{:S(2)}) copy-start(f32[128,8]{0,1:T(8,128)} %param.11) | copy-start | bytes 12292
  262.7 10.9 %copy-start.3 = (bf16[128,2048]{1,0:T(8,128)(2,1)S(1)}, bf16[128,2048]{1,0:T(8,128)(2,1)}, u32[]{:S(2)}) copy-start(bf16[128,2048]{1,0:T(8,128)(2,1)} %param.14) | copy-start | bytes 1572868
  262.7 84.0 %all-to-all-start.2 = ((bf16[64,18,1024]{2,1,0:T(8,128)(2,1)}), bf16[64,18,1024]{2,1,0:T(8,128)(2,1)}, u32[]{:S(2)}, u32[]{:S(2)}) async-start(bf16[64,18,1024]{2,1,0:T(8,128)(2,1)} %copy.39), calls=%async_computation.2 | async-start | bytes 6291456 | tf_op jit(solution)/shard_map/all_to_all | solution.py:66
  273.5 114.7 %all-gather.11.cloned.1.call-start = ((), (), s32[]{:S(2)}) async-start(), calls=%async_computation.7 | async-start | bytes 2621440 | tf_op jit(solution)/shard_map/all_gather | solution.py:10
  346.7 9.5 %copy-start.2 = (bf16[2048,1024]{1,0:T(8,128)(2,1)S(1)}, bf16[2048,1024]{1,0:T(8,128)(2,1)}, u32[]{:S(2)}) copy-start(bf16[2048,1024]{1,0:T(8,128)(2,1)} %param.16) | copy-start | bytes 12582916
  351.5 4.7 copy-start.5
  359.4 185.5 %reduce-scatter.2.cloned.1.call-start = ((), (), s32[]{:S(2)}) async-start(), calls=%async_computation.4 | async-start | bytes 8519680 | tf_op jit(solution)/shard_map/reduce_scatter | solution.py:85
  388.2 158.3 %copy-start.1 = (bf16[128,4096]{1,0:T(8,128)(2,1)S(1)}, bf16[128,4096]{1,0:T(8,128)(2,1)}, u32[]{:S(2)}) copy-start(bf16[128,4096]{1,0:T(8,128)(2,1)} %param.9) | copy-start | bytes 3145732
  388.2 156.7 %copy-start.6 = (f32[32,1024]{1,0:T(8,128)S(1)}, f32[32,1024]{1,0:T(8,128)}, u32[]{:S(2)}) copy-start(f32[32,1024]{1,0:T(8,128)} %param.17) | copy-start | bytes 393220
Sparse Core Ops, SparseCore 0:
  98.2 92.1 all-gather.6
  200.5 53.4 all-gather.8
  359.5 28.6 all-gather.10
  392.3 152.5 reduce-scatter.1
